TPU v7x, 32 devices: a whole 2x2x4 slice. The times are simulated.
32 devices in a mesh: wide: 8 (over z, core), narrow: 4 (over y, x).
Axes of the slice: x: 2, y: 2, z: 4, core: 2. Of those that a mesh axis runs over, the one named last changes fastest.
Arguments:
- inputs: bfloat16 [1, 4096, 4096], P(None, 'narrow', 'wide'), may hold values from -6 to 6
- out_cotangent: bfloat16 [1, 1, 4096, 14336], P(None, None, ('wide', 'narrow')), may hold values from -0.0014648438 to 0.0014648438
- sign_bits: int32 [1, 4096, 16384], P(None, 'wide', 'narrow'), may hold values 0 or 1
- row_pick: int32 [1, 8192], replicated, may hold values from 0 to 4095
- col_pick: int32 [1, 8192], replicated, may hold values from 0 to 16383
Outputs:
- sketch: float32 [1, 1, 8192], P(None, None, ('wide', 'narrow'))
All inputs are finite; a program needn't handle non-finite values. No bound on the sum of `sign_bits` on one device may be relied on, other than what follows from the above.
Results may differ from a plain program's by a relative error of at most 0.0003.
Values may be sent and summed in bfloat16 or wider, within the bound.
No kernel may reach another device: no remote copies, remote signals or barrier semaphores. Data moves between devices by JAX's collectives and lax.ppermute only.
A program may use at most 128 MiB of HBM per device.

v0:
```python
import functools

import jax
import jax.numpy as jnp
import numpy as np
from jax import lax
from jax.experimental import pallas as pl
from jax.experimental.pallas import tpu as pltpu
from jax.sharding import Mesh, PartitionSpec as P

LANES = 128
UNITS = 8
MIB = 1024 * 1024
ALL_AXES = ("hi", "zl", "core", "narrow")


def hadamard(length):
    h = np.ones((1, 1), np.float32)
    while h.shape[0] < length:
        h = np.block([[h, h], [h, -h]])
    return h


def butterfly(parts):
    step = 1
    while step < len(parts):
        parts = [
            parts[i] + parts[i ^ step] if not i & step else parts[i ^ step] - parts[i]
            for i in range(len(parts))
        ]
        step *= 2
    return parts


def plan_chunks(col_dev):
    tile = max(LANES, min(256, col_dev // UNITS))
    units = col_dev // tile
    middle = (units - 2) // 2
    return tile, [1, units - 2 - middle, middle, 1]


def prep_kernel(real_blocks, zl_count, widths, in_ref, *out_refs):
    block = pl.program_id(1) * zl_count + pl.program_id(0)
    keep = block < real_blocks
    start = 0
    for width, out_ref in zip(widths, out_refs):
        value = in_ref[:, start : start + width]
        out_ref[0] = jnp.where(keep, value, jnp.zeros_like(value))
        start += width


def prepare(cot, zl_count, narrow_count, widths):
    tokens, hidden = cot.shape
    col_dev = sum(widths)
    real_blocks = hidden // col_dev
    return pl.pallas_call(
        functools.partial(prep_kernel, real_blocks, zl_count, widths),
        grid=(zl_count, narrow_count),
        in_specs=[
            pl.BlockSpec(
                (tokens, col_dev),
                lambda z, n: (0, jnp.minimum(n * zl_count + z, real_blocks - 1)),
            )
        ],
        out_specs=[
            pl.BlockSpec((1, tokens, width), lambda z, n: (z * narrow_count + n, 0, 0))
            for width in widths
        ],
        out_shape=[
            jax.ShapeDtypeStruct((zl_count * narrow_count, tokens, width), cot.dtype)
            for width in widths
        ],
        compiler_params=pltpu.CompilerParams(vmem_limit_bytes=60 * MIB),
        cost_estimate=pl.CostEstimate(
            flops=0, bytes_accessed=4 * cot.size, transcendentals=0
        ),
        name="cut_columns",
    )(cot)


def chunk_kernel(hi_count, zl_count, place_ref, *refs):
    xt = refs[:zl_count]
    cots = refs[zl_count : zl_count + 2 * hi_count]
    signs = refs[zl_count + 2 * hi_count : 2 * zl_count + 2 * hi_count]
    row_mix = refs[-2]
    out_ref = refs[-1]
    hi, core = place_ref[0], place_ref[2]
    mixed = []
    for d in range(zl_count):
        total = None
        for h in range(hi_count):
            for c in range(2):
                for z in range(zl_count):
                    source = ((hi ^ h) * zl_count + z) * 2 + (core ^ c)
                    term = jnp.dot(
                        xt[d][source],
                        cots[h * 2 + c][z],
                        preferred_element_type=jnp.float32,
                    )
                    total = term if total is None else total + term
        value = total * signs[d][...].astype(jnp.float32)
        high = value.astype(jnp.bfloat16)
        low = (value - high.astype(jnp.float32)).astype(jnp.bfloat16)
        mixed.append(
            jnp.dot(row_mix[...], high, preferred_element_type=jnp.float32)
            + jnp.dot(row_mix[...], low, preferred_element_type=jnp.float32)
        )
    mixed = butterfly(mixed)
    for b in range(out_ref.shape[0]):
        for d in range(zl_count):
            out_ref[b, d] = mixed[d][:, b * LANES : (b + 1) * LANES]


def chunk_call(place, xt, cots, signs, row_mix, tile, steps, hi_count):
    zl_count = len(xt)
    sources, rows, tokens = xt[0].shape
    chunk = tile * steps
    resident = pl.Buffered(1)
    return pl.pallas_call(
        functools.partial(chunk_kernel, hi_count, zl_count),
        grid_spec=pltpu.PrefetchScalarGridSpec(
            num_scalar_prefetch=1,
            grid=(steps,),
            in_specs=[
                pl.BlockSpec(
                    (sources, rows, tokens), lambda i, p: (0, 0, 0), pipeline_mode=resident
                )
                for _ in xt
            ]
            + [
                pl.BlockSpec((zl_count, tokens, tile), lambda i, p: (0, 0, i))
                for _ in cots
            ]
            + [
                pl.BlockSpec((rows, tile), lambda i, p: (0, i))
                for _ in signs
            ]
            + [
                pl.BlockSpec((rows, rows), lambda i, p: (0, 0), pipeline_mode=resident)
            ],
            out_specs=pl.BlockSpec(
                (tile // LANES, zl_count, rows, LANES), lambda i, p: (i, 0, 0, 0)
            ),
        ),
        out_shape=jax.ShapeDtypeStruct(
            (chunk // LANES, zl_count, rows, LANES), jnp.float32
        ),
        compiler_params=pltpu.CompilerParams(vmem_limit_bytes=40 * MIB),
        cost_estimate=pl.CostEstimate(
            flops=zl_count * rows * chunk * tokens,
            bytes_accessed=4 * zl_count * rows * chunk,
            transcendentals=0,
        ),
        name="gradient_rows",
    )(place, *xt, *cots, *signs, row_mix)


def pick_kernel(parts, index_ref, *refs):
    blocks = refs[:parts]
    lane_signs, out_ref, mixed_ref, rows_ref = refs[parts:]
    rows = blocks[0].shape[1]
    slabs = [(block, b) for block in blocks for b in range(block.shape[0])]

    def mix(i, carry):
        spot = pl.ds(pl.multiple_of(i * 8, 8), 8)
        values = [block[b, spot, :] for block, b in slabs]
        for b, value in enumerate(butterfly(values)):
            mixed_ref[pl.ds(pl.multiple_of(b * rows + i * 8, 8), 8), :] = value
        return carry

    lax.fori_loop(0, rows // 8, mix, 0)

    def gather(g, carry):
        for j in range(LANES):
            row = index_ref[g * LANES + j]
            rows_ref[g, j : j + 1, :] = mixed_ref[pl.ds(row, 1), :]
        return carry

    groups = out_ref.shape[0]
    lax.fori_loop(0, groups, gather, 0)
    side = 4 if groups % 4 == 0 else 1

    def reduce(i, carry):
        for q in range(side):
            g = i * side + q
            spot = pl.ds(pl.multiple_of(g * LANES, LANES), LANES)
            product = rows_ref[g] * lane_signs[spot, :].astype(jnp.float32)
            out_ref[pl.ds(g, 1), :] = jnp.sum(product.T, axis=0, keepdims=True)
        return carry

    lax.fori_loop(0, groups // side, reduce, 0)


def pick_call(index, blocks, lane_signs):
    picks = index.shape[0]
    total = sum(block.shape[0] * block.shape[1] for block in blocks)
    return pl.pallas_call(
        functools.partial(pick_kernel, len(blocks)),
        grid_spec=pltpu.PrefetchScalarGridSpec(
            num_scalar_prefetch=1,
            grid=(1,),
            in_specs=[
                pl.BlockSpec(
                    block.shape, lambda i, p: (0, 0, 0), pipeline_mode=pl.Buffered(1)
                )
                for block in blocks
            ]
            + [
                pl.BlockSpec(
                    (picks, LANES), lambda i, p: (0, 0), pipeline_mode=pl.Buffered(1)
                )
            ],
            out_specs=pl.BlockSpec((picks // LANES, LANES), lambda i, p: (0, 0)),
            scratch_shapes=[
                pltpu.VMEM((total, LANES), jnp.float32),
                pltpu.VMEM((picks // LANES, LANES, LANES), jnp.float32),
            ],
        ),
        out_shape=jax.ShapeDtypeStruct((picks // LANES, LANES), jnp.float32),
        compiler_params=pltpu.CompilerParams(vmem_limit_bytes=40 * MIB),
        cost_estimate=pl.CostEstimate(
            flops=8 * total * LANES, bytes_accessed=4 * total * LANES, transcendentals=0
        ),
        name="pick_samples",
    )(index, *blocks, lane_signs)


def parity_sign(bits):
    for shift in (16, 8, 4, 2, 1):
        bits = bits ^ (bits >> shift)
    return 1 - 2 * (bits & 1)


def swap(value, axis, offset):
    count = lax.axis_size(axis)
    return lax.ppermute(value, axis, [(i, i ^ offset) for i in range(count)])


def after(value, *others):
    return lax.optimization_barrier((value, *others))[0]


def body(inputs, out_cotangent, sign_bits, row_pick, col_pick):
    hi_count = lax.axis_size("hi")
    zl_count = lax.axis_size("zl")
    narrow_count = lax.axis_size("narrow")
    hi, zl, core, narrow = [lax.axis_index(a) for a in ALL_AXES]
    wide_count = hi_count * zl_count * 2
    token_shard, rows = inputs.shape[1:]
    col_shard = sign_bits.shape[2]
    col_dev = col_shard // zl_count
    tile, chunks = plan_chunks(col_dev)
    tokens = token_shard * narrow_count // wide_count
    cut = prepare(
        out_cotangent[0, 0], zl_count, narrow_count, [tile * steps for steps in chunks]
    )

    own_xt = inputs[0].reshape(token_shard // tokens, tokens, rows).swapaxes(1, 2)
    xt_parts = [swap(own_xt, "zl", d) if d else own_xt for d in range(zl_count)]

    row_mix = jnp.asarray(hadamard(rows), jnp.bfloat16)
    place = jnp.stack([hi, zl, core]).astype(jnp.int32)
    edges = [tile * sum(chunks[:i]) for i in range(len(chunks) + 1)]
    count = len(chunks)
    own, far, signs, swapped = {}, {}, {}, {}
    blocks, xt = [], None
    cut = list(cut)
    bits = sign_bits[0]
    samples = (row_pick[0], col_pick[0])

    def sign_block(d, index):
        start = (zl ^ d) * col_dev + edges[index]
        part = lax.dynamic_slice_in_dim(bits, start, tile * chunks[index], axis=1)
        return (2 * part - 1).astype(jnp.bfloat16)

    for stage in range(count + 2):
        if stage < count:
            signs[stage] = [sign_block(d, stage) for d in range(zl_count)]
            part = after(cut[stage], *signs[stage]) if stage > 1 else cut[stage]
            own[stage] = lax.all_to_all(part, ("zl", "narrow"), 0, 0, tiled=True)
        if 1 <= stage <= count:
            c = stage - 1
            far[c] = [swap(own[c], "hi", h) for h in range(1, hi_count)]
            swapped[c] = [swap(own[c], "core", 1)]
            signs[c] = [swap(x, "zl", d) if d else x for d, x in enumerate(signs[c])]
        if stage >= 2:
            c = stage - 2
            swapped[c] += [swap(x, "core", 1) for x in far[c]]
        ready = {count - 1: range(count - 2), count: [count - 2], count + 1: [count - 1]}
        for c in ready.get(stage, []):
            pairs = zip([own[c]] + far[c], swapped[c])
            cots = [
                x.reshape(zl_count, tokens, tile * chunks[c]) for pair in pairs for x in pair
            ]
            done = chunk_call(
                place, xt, cots, signs[c], row_mix, tile, chunks[c], hi_count
            )
            blocks.append(done.reshape(-1, zl_count * rows, LANES))
            place = after(place, done)
        if stage == 2:
            row, col = samples
            block = (col // LANES) % (col_dev // LANES)
            row_in = (row // (2 * rows)) % zl_count * rows + row % rows
            position = block * (zl_count * rows) + row_in
            row_base = ((hi * zl_count + zl) * 2 + core) * rows
            col_base = narrow * col_shard + zl * col_dev
            lane = lax.broadcasted_iota(jnp.int32, (1, LANES), 1)
            fold = parity_sign((row & row_base)[:, None]) * parity_sign((col_base + lane) & col[:, None])
            samples = (position, fold.astype(jnp.bfloat16))
        state = (cut, own, far, signs, swapped, blocks, bits, place, xt_parts, samples)
        state = lax.optimization_barrier(state)
        cut, own, far, signs, swapped, blocks, bits, place, xt_parts, samples = state
        if stage == 0:
            xt = [lax.all_gather(x, "narrow", axis=0, tiled=True) for x in [own_xt] + xt_parts[1:]]
    position, lane_signs = samples
    picked = pick_call(position, blocks, lane_signs)

    devices = wide_count * narrow_count
    terms = lax.all_to_all(
        picked.reshape(devices, position.shape[0] // devices), ALL_AXES, 0, 0, tiled=True
    )
    total = jnp.sum(terms, axis=0) / jnp.sqrt(jnp.float32(position.shape[0]))
    return total.reshape(1, 1, -1)


def solution(mesh):
    wide, narrow = mesh.shape["wide"], mesh.shape["narrow"]
    sizes = (2, wide // 4, 2, narrow)
    split = Mesh(mesh.devices.reshape(sizes), ALL_AXES)
    wide_axes = ("hi", "zl", "core")
    return jax.shard_map(
        body,
        mesh=split,
        in_specs=(
            P(None, "narrow", wide_axes),
            P(None, None, ALL_AXES, None),
            P(None, wide_axes, "narrow"),
            P(),
            P(),
        ),
        out_specs=P(None, None, ALL_AXES),
        check_vma=False,
    )
```

profile of v0, /device:TPU:0, one launch (start us, length us, event | category | flops | bytes accessed | tf_op | source)
XLA Modules:
  0.0 308.0 jit_solution(15389638244342325293)
XLA Ops:
  8.9 3.1 %collective-permute-start = (bf16[2,512,512]{1,2,0:T(8,128)(2,1)}, bf16[2,512,512]{1,2,0:T(8,128)(2,1)}, u32[]{:S(2)}, u32[]{:S(2)}) collective-permute-start(bf16[2,512,512]{1,2,0:T(8,128)(2,1)} %bitcast.57), channel_id=1, source_target_pairs={{0,8},{8,0},{1,9},{9,1},{2,10},{10,2},{3,11},{11,3},{4,12},{12,4},... | collective-permute-start | bytes 3145736 | tf_op jit(solution)/shard_map/ppermute | solution.py:236
  11.9 6.7 %cut_columns.1 = (bf16[8,128,256]{2,1,0:T(8,128)(2,1)}, bf16[8,128,768]{2,1,0:T(8,128)(2,1)}, bf16[8,128,768]{2,1,0:T(8,128)(2,1)}, bf16[8,128,256]{2,1,0:T(8,128)(2,1)}) custom-call(bf16[128,14336]{1,0:T(8,128)(2,1)} %bitcast.55), custom_call_target="tpu_custom_call" | custom-call | bytes 7340032 | tf_op jit(solution)/shard_map/cut_columns/pallas_call | solution.py:56
  18.7 3.7 %all-to-all-start = ((bf16[8,128,256]{2,1,0:T(8,128)(2,1)}), bf16[8,128,256]{2,1,0:T(8,128)(2,1)S(1)}, u32[]{:S(2)}, u32[]{:S(2)}) async-start(bf16[8,128,256]{2,1,0:T(8,128)(2,1)} %get-tuple-element.88), calls=%async_computation | async-start | bytes 1048576 | tf_op jit(solution)/shard_map/all_to_all | solution.py:280
  24.5 17.8 %all-to-all-done = bf16[8,128,256]{2,1,0:T(8,128)(2,1)S(1)} async-done(((bf16[8,128,256]{2,1,0:T(8,128)(2,1)}), bf16[8,128,256]{2,1,0:T(8,128)(2,1)S(1)}, u32[]{:S(2)}, u32[]{:S(2)}) %all-to-all-start) | async-done | bytes 524320 | tf_op jit(solution)/shard_map/all_to_all | solution.py:280
  42.3 3.7 %all-to-all-start.1 = ((bf16[8,128,768]{2,1,0:T(8,128)(2,1)}), bf16[8,128,768]{2,1,0:T(8,128)(2,1)S(1)}, u32[]{:S(2)}, u32[]{:S(2)}) async-start(bf16[8,128,768]{2,1,0:T(8,128)(2,1)} %get-tuple-element.92), calls=%async_computation.1 | async-start | bytes 3145728 | tf_op jit(solution)/shard_map/all_to_all | solution.py:280
  48.4 2.6 collective-permute-start.1
  52.9 3.4 %add_convert_fusion.2 = (bf16[512,768]{1,0:T(8,128)(2,1)}, bf16[512,768]{1,0:T(8,128)(2,1)}) fusion(s32[512,4096]{1,0:T(8,128)} %bitcast.52, s32[]{:T(128)S(6)} %select_n.50, s32[]{:T(128)S(6)} %select_n.49), kind=kLoop, calls=%fused_computation.12 | loop fusion | flops 2359296 | bytes 4718600 | tf_op jit(solution)/shard_map/convert_element_type | solution.py:274
  56.4 24.8 %collective-permute-done.2.refs_7_ = bf16[512,256]{1,0:T(8,128)(2,1)} collective-permute-done((bf16[512,256]{1,0:T(8,128)(2,1)}, bf16[512,256]{1,0:T(8,128)(2,1)}, u32[]{:S(2)}, u32[]{:S(2)}) %collective-permute-start.2) | collective-permute-done | bytes 262176 | tf_op jit(solution)/shard_map/ppermute | solution.py:236
  81.2 4.4 %add_convert_fusion = (bf16[512,768]{1,0:T(8,128)(2,1)}, bf16[512,768]{1,0:T(8,128)(2,1)}) fusion(s32[512,4096]{1,0:T(8,128)} %bitcast.53, s32[]{:T(128)S(6)} %select_n.52, s32[]{:T(128)S(6)} %select_n.51), kind=kLoop, calls=%fused_computation.10 | loop fusion | flops 2359296 | bytes 4718600 | tf_op jit(solution)/shard_map/convert_element_type | solution.py:274
  85.6 4.4 %all-to-all-start.2 = ((bf16[8,128,768]{2,1,0:T(8,128)(2,1)}), bf16[8,128,768]{2,1,0:T(8,128)(2,1)}, u32[]{:S(2)}, u32[]{:S(2)}) async-start(bf16[8,128,768]{2,1,0:T(8,128)(2,1)} %get-tuple-element.108), calls=%async_computation.2 | async-start | bytes 3145728 | tf_op jit(solution)/shard_map/all_to_all | solution.py:280
  90.2 2.7 collective-permute-start.4
  94.9 4.7 %fusion.4.refs_4_ = bf16[8192,128]{1,0:T(8,128)(2,1)} fusion(s32[8192]{0:T(1024)S(1)} %bitcast.59, s32[128]{0:T(128)S(1)} %iota_add_fusion, s32[8192]{0:T(1024)S(1)} %get-tuple-element.179), kind=kLoop, calls=%fused_computation.9 | loop fusion | flops 16777216 | bytes 2163200 | tf_op jit(solution)/shard_map/convert_element_type | solution.py:309
  100.5 55.6 %collective-permute-done.5.refs_7_ = bf16[512,768]{1,0:T(8,128)(2,1)S(1)} collective-permute-done((bf16[512,768]{1,0:T(8,128)(2,1)}, bf16[512,768]{1,0:T(8,128)(2,1)S(1)}, u32[]{:S(2)}, u32[]{:S(2)}) %collective-permute-start.5) | collective-permute-done | bytes 786464 | tf_op jit(solution)/shard_map/ppermute | solution.py:236
  158.1 3.6 %collective-permute-done.4 = bf16[8,128,768]{2,1,0:T(8,128)(2,1)} collective-permute-done((bf16[8,128,768]{2,1,0:T(8,128)(2,1)S(1)}, bf16[8,128,768]{2,1,0:T(8,128)(2,1)}, u32[]{:S(2)}, u32[]{:S(2)}) %collective-permute-start.4) | collective-permute-done | bytes 1572896 | tf_op jit(solution)/shard_map/ppermute | solution.py:236
  165.4 6.4 %all-to-all-start.3 = ((bf16[8,128,256]{2,1,0:T(8,128)(2,1)}), bf16[8,128,256]{2,1,0:T(8,128)(2,1)}, u32[]{:S(2)}, u32[]{:S(2)}) async-start(bf16[8,128,256]{2,1,0:T(8,128)(2,1)} %get-tuple-element.123), calls=%async_computation.3 | async-start | bytes 1048576 | tf_op jit(solution)/shard_map/all_to_all | solution.py:280
  181.4 7.4 %gradient_rows.4 = f32[2,2,512,128]{3,2,1,0:T(8,128)S(1)} custom-call(s32[3]{0:T(128)S(1)} %pad_add_fusion.place_ref, bf16[8,512,512]{2,1,0:T(8,128)(2,1)S(1)} %copy-done, bf16[8,512,512]{2,1,0:T(8,128)(2,1)S(1)} %copy-done.2, bf16[2,512,256]{2,1,0:T(8,128)(2,1)S(1)} %bitcast.41, bf16[2,512,256]{2,1,0:T(8,128)(2,1)S(1)} %bitcast.45, ...), custom_call_target="tpu_custom_call" | custom-call | flops 134217728 | bytes 1048576 | tf_op jit(solution)/shard_map/gradient_rows/pallas_call | solution.py:119
  191.5 21.5 %gradient_rows.5 = f32[6,2,512,128]{3,2,1,0:T(8,128)S(1)} custom-call(s32[3]{0:T(128)S(1)} %pad_add_fusion.place_ref, bf16[8,512,512]{2,1,0:T(8,128)(2,1)} %all-gather.3.cloned.1.call-done.refs_0_, bf16[8,512,512]{2,1,0:T(8,128)(2,1)} %all-gather.5.cloned.1.call-done.refs_1_, bf16[2,512,768]{2,1,0:T(8,128)(2,1)S(1)} %bitcast.38, ...), custom_call_target="tpu_custom_call" | custom-call | flops 402653184 | bytes 3145728 | tf_op jit(solution)/shard_map/gradient_rows/pallas_call | solution.py:119
  212.9 7.2 %collective-permute-done.9.refs_7_ = bf16[512,768]{1,0:T(8,128)(2,1)} collective-permute-done((bf16[512,768]{1,0:T(8,128)(2,1)}, bf16[512,768]{1,0:T(8,128)(2,1)}, u32[]{:S(2)}, u32[]{:S(2)}) %collective-permute-start.9) | collective-permute-done | bytes 786464 | tf_op jit(solution)/shard_map/ppermute | solution.py:236
  220.1 13.4 %collective-permute-done.8 = bf16[8,128,768]{2,1,0:T(8,128)(2,1)} collective-permute-done((bf16[8,128,768]{2,1,0:T(8,128)(2,1)}, bf16[8,128,768]{2,1,0:T(8,128)(2,1)}, u32[]{:S(2)}, u32[]{:S(2)}) %collective-permute-start.8) | collective-permute-done | bytes 1572896 | tf_op jit(solution)/shard_map/ppermute | solution.py:236
  234.0 2.7 collective-permute-start.13
  241.9 21.9 %gradient_rows.6 = f32[6,2,512,128]{3,2,1,0:T(8,128)S(1)} custom-call(s32[3]{0:T(128)S(1)} %pad_add_fusion.place_ref, bf16[8,512,512]{2,1,0:T(8,128)(2,1)} %all-gather.3.cloned.1.call-done.refs_0_, bf16[8,512,512]{2,1,0:T(8,128)(2,1)} %all-gather.5.cloned.1.call-done.refs_1_, bf16[2,512,768]{2,1,0:T(8,128)(2,1)} %bitcast.22.refs_2_, ...), custom_call_target="tpu_custom_call" | custom-call | flops 402653184 | bytes 3145728 | tf_op jit(solution)/shard_map/gradient_rows/pallas_call | solution.py:119
  269.0 7.5 %gradient_rows.7 = f32[2,2,512,128]{3,2,1,0:T(8,128)S(1)} custom-call(s32[3]{0:T(128)S(1)} %pad_add_fusion.place_ref, bf16[8,512,512]{2,1,0:T(8,128)(2,1)S(1)} %copy-done.1, bf16[8,512,512]{2,1,0:T(8,128)(2,1)S(1)} %copy-done.3, bf16[2,512,256]{2,1,0:T(8,128)(2,1)} %bitcast.27.refs_2_, bf16[2,512,256]{2,1,0:T(8,128)(2,1)S(1)} %bitcast.48, ...), custom_call_target="tpu_custom_call" | custom-call | flops 134217728 | bytes 1048576 | tf_op jit(solution)/shard_map/gradient_rows/pallas_call | solution.py:119
  276.6 12.6 %pick_samples.1 = f32[64,128]{1,0:T(8,128)S(1)} custom-call(s32[8192]{0:T(1024)S(1)} %get-tuple-element.165.index_ref, f32[2,1024,128]{2,1,0:T(8,128)S(1)} %bitcast.39, f32[6,1024,128]{2,1,0:T(8,128)S(1)} %bitcast.36, f32[6,1024,128]{2,1,0:T(8,128)S(1)} %bitcast.37, f32[2,1024,128]{2,1,0:T(8,128)S(1)} %bitcast.40, bf16[8192,128]{1,0:T(8,128)(2,1)S(1)} %copy-done.9), custom_call_target="tpu_custom_call" | custom-call | flops 16777216 | bytes 8388608 | tf_op jit(solution)/shard_map/pick_samples/pallas_call | solution.py:197
  289.2 11.4 %all_to_all.29 = f32[32,1,256]{2,1,0:T(1,128)S(1)} all-to-all(f32[32,1,256]{2,1,0:T(1,128)S(1)} %bitcast.51), channel_id=1, replica_groups=mesh['hi'=2,'zl'=2,'core'=2,'narrow'=4] {'hi','zl','core','narrow'}, dimensions={0} | all-to-all | bytes 65536 | tf_op jit(solution)/shard_map/all_to_all | solution.py:319
  (111 shorter events, 41.2 us)
Async XLA Ops:
  6.5 167.3 %all-gather.3.cloned.1.call-start = ((), (), s32[]{:S(2)}) async-start(), calls=%async_computation.5 | async-start | bytes 5242880 | tf_op jit(solution)/shard_map/all_gather | solution.py:314
  8.9 33.4 %collective-permute-start = (bf16[2,512,512]{1,2,0:T(8,128)(2,1)}, bf16[2,512,512]{1,2,0:T(8,128)(2,1)}, u32[]{:S(2)}, u32[]{:S(2)}) collective-permute-start(bf16[2,512,512]{1,2,0:T(8,128)(2,1)} %bitcast.57), channel_id=1, source_target_pairs={{0,8},{8,0},{1,9},{9,1},{2,10},{10,2},{3,11},{11,3},{4,12},{12,4},... | collective-permute-start | bytes 3145736 | tf_op jit(solution)/shard_map/ppermute | solution.py:236
  18.7 23.6 %all-to-all-start = ((bf16[8,128,256]{2,1,0:T(8,128)(2,1)}), bf16[8,128,256]{2,1,0:T(8,128)(2,1)S(1)}, u32[]{:S(2)}, u32[]{:S(2)}) async-start(bf16[8,128,256]{2,1,0:T(8,128)(2,1)} %get-tuple-element.88), calls=%async_computation | async-start | bytes 1048576 | tf_op jit(solution)/shard_map/all_to_all | solution.py:280
  42.3 38.9 %all-to-all-start.1 = ((bf16[8,128,768]{2,1,0:T(8,128)(2,1)}), bf16[8,128,768]{2,1,0:T(8,128)(2,1)S(1)}, u32[]{:S(2)}, u32[]{:S(2)}) async-start(bf16[8,128,768]{2,1,0:T(8,128)(2,1)} %get-tuple-element.92), calls=%async_computation.1 | async-start | bytes 3145728 | tf_op jit(solution)/shard_map/all_to_all | solution.py:280
  46.0 127.9 %all-gather.5.cloned.1.call-start = ((), (), s32[]{:S(2)}) async-start(), calls=%async_computation.6 | async-start | bytes 5242880 | tf_op jit(solution)/shard_map/all_gather | solution.py:314
  48.3 32.9 %collective-permute-start.3 = (bf16[8,128,256]{2,1,0:T(8,128)(2,1)S(1)}, bf16[8,128,256]{2,1,0:T(8,128)(2,1)S(1)}, u32[]{:S(2)}, u32[]{:S(2)}) collective-permute-start(bf16[8,128,256]{2,1,0:T(8,128)(2,1)S(1)} %all-to-all-done), channel_id=1, source_target_pairs={{0,4},{4,0},{1,5},{5,1},{2,6},{6,2},{3,7},{7,3},{8,12},{12,8},{9,1... | collective-permute-start | bytes 1572872 | tf_op jit(solution)/shard_map/ppermute | solution.py:236
  48.4 32.8 %collective-permute-start.1 = (bf16[8,128,256]{2,1,0:T(8,128)(2,1)S(1)}, bf16[8,128,256]{2,1,0:T(8,128)(2,1)S(1)}, u32[]{:S(2)}, u32[]{:S(2)}) collective-permute-start(bf16[8,128,256]{2,1,0:T(8,128)(2,1)S(1)} %all-to-all-done), channel_id=1, source_target_pairs={{0,16},{16,0},{1,17},{17,1},{2,18},{18,2},{3,19},{19,3},{4,20},{20... | collective-permute-start | bytes 1572872 | tf_op jit(solution)/shard_map/ppermute | solution.py:236
  51.0 30.1 %collective-permute-start.2 = (bf16[512,256]{1,0:T(8,128)(2,1)}, bf16[512,256]{1,0:T(8,128)(2,1)}, u32[]{:S(2)}, u32[]{:S(2)}) collective-permute-start(bf16[512,256]{1,0:T(8,128)(2,1)} %get-tuple-element.97), channel_id=1, source_target_pairs={{0,8},{8,0},{1,9},{9,1},{2,10},{10,2},{3,11},{11,3},{4,12},{12,4},... | collective-permute-start | bytes 786440 | tf_op jit(solution)/shard_map/ppermute | solution.py:236
  85.6 88.2 %copy-start.6 = (bf16[512,512]{1,0:T(8,128)(2,1)S(1)}, bf16[512,512]{1,0:T(8,128)(2,1)}, u32[]{:S(2)}) copy-start(bf16[512,512]{1,0:T(8,128)(2,1)} %constant.133.clone.refs_8_) | copy-start | bytes 1572868
  85.6 76.1 %all-to-all-start.2 = ((bf16[8,128,768]{2,1,0:T(8,128)(2,1)}), bf16[8,128,768]{2,1,0:T(8,128)(2,1)}, u32[]{:S(2)}, u32[]{:S(2)}) async-start(bf16[8,128,768]{2,1,0:T(8,128)(2,1)} %get-tuple-element.108), calls=%async_computation.2 | async-start | bytes 3145728 | tf_op jit(solution)/shard_map/all_to_all | solution.py:280
  90.1 66.9 %collective-permute-start.7 = (bf16[8,128,768]{2,1,0:T(8,128)(2,1)S(1)}, bf16[8,128,768]{2,1,0:T(8,128)(2,1)S(1)}, u32[]{:S(2)}, u32[]{:S(2)}) collective-permute-start(bf16[8,128,768]{2,1,0:T(8,128)(2,1)S(1)} %all-to-all-done.1), channel_id=1, source_target_pairs={{0,4},{4,0},{1,5},{5,1},{2,6},{6,2},{3,7},{7,3},{8,12},{12,8},{9,1... | collective-permute-start | bytes 4718600 | tf_op jit(solution)/shard_map/ppermute | solution.py:236
  90.2 71.6 %collective-permute-start.4 = (bf16[8,128,768]{2,1,0:T(8,128)(2,1)S(1)}, bf16[8,128,768]{2,1,0:T(8,128)(2,1)}, u32[]{:S(2)}, u32[]{:S(2)}) collective-permute-start(bf16[8,128,768]{2,1,0:T(8,128)(2,1)S(1)} %all-to-all-done.1), channel_id=1, source_target_pairs={{0,16},{16,0},{1,17},{17,1},{2,18},{18,2},{3,19},{19,3},{4,20},{20... | collective-permute-start | bytes 4718600 | tf_op jit(solution)/shard_map/ppermute | solution.py:236
  92.8 6.8 %collective-permute-start.6 = (bf16[8,128,256]{2,1,0:T(8,128)(2,1)S(1)}, bf16[8,128,256]{2,1,0:T(8,128)(2,1)S(1)}, u32[]{:S(2)}, u32[]{:S(2)}) collective-permute-start(bf16[8,128,256]{2,1,0:T(8,128)(2,1)S(1)} %collective-permute-done.1), channel_id=1, source_target_pairs={{0,4},{4,0},{1,5},{5,1},{2,6},{6,2},{3,7},{7,3},{8,12},{12,8},{9,1... | collective-permute-start | bytes 1572872 | tf_op jit(solution)/shard_map/ppermute | solution.py:236
  93.0 63.1 %collective-permute-start.5 = (bf16[512,768]{1,0:T(8,128)(2,1)}, bf16[512,768]{1,0:T(8,128)(2,1)S(1)}, u32[]{:S(2)}, u32[]{:S(2)}) collective-permute-start(bf16[512,768]{1,0:T(8,128)(2,1)} %get-tuple-element.113), channel_id=1, source_target_pairs={{0,8},{8,0},{1,9},{9,1},{2,10},{10,2},{3,11},{11,3},{4,12},{12,4},... | collective-permute-start | bytes 2359304 | tf_op jit(solution)/shard_map/ppermute | solution.py:236
  161.7 27.1 %collective-permute-start.10 = (bf16[8,128,768]{2,1,0:T(8,128)(2,1)}, bf16[8,128,768]{2,1,0:T(8,128)(2,1)S(1)}, u32[]{:S(2)}, u32[]{:S(2)}) collective-permute-start(bf16[8,128,768]{2,1,0:T(8,128)(2,1)} %collective-permute-done.4), channel_id=1, source_target_pairs={{0,4},{4,0},{1,5},{5,1},{2,6},{6,2},{3,7},{7,3},{8,12},{12,8},{9,1... | collective-permute-start | bytes 4718600 | tf_op jit(solution)/shard_map/ppermute | solution.py:236
  161.7 58.4 %collective-permute-start.11 = (bf16[8,128,768]{2,1,0:T(8,128)(2,1)}, bf16[8,128,768]{2,1,0:T(8,128)(2,1)}, u32[]{:S(2)}, u32[]{:S(2)}) collective-permute-start(bf16[8,128,768]{2,1,0:T(8,128)(2,1)} %all-to-all-done.2), channel_id=1, source_target_pairs={{0,4},{4,0},{1,5},{5,1},{2,6},{6,2},{3,7},{7,3},{8,12},{12,8},{9,1... | collective-permute-start | bytes 4718600 | tf_op jit(solution)/shard_map/ppermute | solution.py:236
  162.3 71.2 %collective-permute-start.8 = (bf16[8,128,768]{2,1,0:T(8,128)(2,1)}, bf16[8,128,768]{2,1,0:T(8,128)(2,1)}, u32[]{:S(2)}, u32[]{:S(2)}) collective-permute-start(bf16[8,128,768]{2,1,0:T(8,128)(2,1)} %all-to-all-done.2), channel_id=1, source_target_pairs={{0,16},{16,0},{1,17},{17,1},{2,18},{18,2},{3,19},{19,3},{4,20},{20... | collective-permute-start | bytes 4718600 | tf_op jit(solution)/shard_map/ppermute | solution.py:236
  165.4 54.7 %all-to-all-start.3 = ((bf16[8,128,256]{2,1,0:T(8,128)(2,1)}), bf16[8,128,256]{2,1,0:T(8,128)(2,1)}, u32[]{:S(2)}, u32[]{:S(2)}) async-start(bf16[8,128,256]{2,1,0:T(8,128)(2,1)} %get-tuple-element.123), calls=%async_computation.3 | async-start | bytes 1048576 | tf_op jit(solution)/shard_map/all_to_all | solution.py:280
  171.8 48.3 %collective-permute-start.9 = (bf16[512,768]{1,0:T(8,128)(2,1)}, bf16[512,768]{1,0:T(8,128)(2,1)}, u32[]{:S(2)}, u32[]{:S(2)}) collective-permute-start(bf16[512,768]{1,0:T(8,128)(2,1)} %get-tuple-element.131), channel_id=1, source_target_pairs={{0,8},{8,0},{1,9},{9,1},{2,10},{10,2},{3,11},{11,3},{4,12},{12,4},... | collective-permute-start | bytes 2359304 | tf_op jit(solution)/shard_map/ppermute | solution.py:236
  233.5 3.6 %collective-permute-start.14 = (bf16[8,128,768]{2,1,0:T(8,128)(2,1)}, bf16[8,128,768]{2,1,0:T(8,128)(2,1)S(1)}, u32[]{:S(2)}, u32[]{:S(2)}) collective-permute-start(bf16[8,128,768]{2,1,0:T(8,128)(2,1)} %collective-permute-done.8), channel_id=1, source_target_pairs={{0,4},{4,0},{1,5},{5,1},{2,6},{6,2},{3,7},{7,3},{8,12},{12,8},{9,1... | collective-permute-start | bytes 4718600 | tf_op jit(solution)/shard_map/ppermute | solution.py:236
  233.5 32.7 %collective-permute-start.15 = (bf16[8,128,256]{2,1,0:T(8,128)(2,1)}, bf16[8,128,256]{2,1,0:T(8,128)(2,1)S(1)}, u32[]{:S(2)}, u32[]{:S(2)}) collective-permute-start(bf16[8,128,256]{2,1,0:T(8,128)(2,1)} %all-to-all-done.3), channel_id=1, source_target_pairs={{0,4},{4,0},{1,5},{5,1},{2,6},{6,2},{3,7},{7,3},{8,12},{12,8},{9,1... | collective-permute-start | bytes 1572872 | tf_op jit(solution)/shard_map/ppermute | solution.py:236
  234.0 32.2 %collective-permute-start.12 = (bf16[8,128,256]{2,1,0:T(8,128)(2,1)}, bf16[8,128,256]{2,1,0:T(8,128)(2,1)S(1)}, u32[]{:S(2)}, u32[]{:S(2)}) collective-permute-start(bf16[8,128,256]{2,1,0:T(8,128)(2,1)} %all-to-all-done.3), channel_id=1, source_target_pairs={{0,16},{16,0},{1,17},{17,1},{2,18},{18,2},{3,19},{19,3},{4,20},{20... | collective-permute-start | bytes 1572872 | tf_op jit(solution)/shard_map/ppermute | solution.py:236
  234.0 31.4 %collective-permute-start.13 = (bf16[512,256]{1,0:T(8,128)(2,1)}, bf16[512,256]{1,0:T(8,128)(2,1)S(1)}, u32[]{:S(2)}, u32[]{:S(2)}) collective-permute-start(bf16[512,256]{1,0:T(8,128)(2,1)} %get-tuple-element.146), channel_id=1, source_target_pairs={{0,8},{8,0},{1,9},{9,1},{2,10},{10,2},{3,11},{11,3},{4,12},{12,4},... | collective-permute-start | bytes 786440 | tf_op jit(solution)/shard_map/ppermute | solution.py:236
  266.2 1.9 collective-permute-start.16
  (33 other events, 215.8 us)
Sparse Core Ops, SparseCore 0:
  9.2 77.3 all-gather.2
  88.5 62.6 all-gather.4
where the time goes:
time: 309 us; the launch traced here: 308 us
  waiting for transfers between devices  125 us (40%)
  Pallas kernels  77.6 us (25%)
  starting transfers between devices  37.6 us (12%)
  local copies, waits for them, and re-layouts  25.6 us (8%)
  other arithmetic  17.4 us (6%)
  between operations  13.7 us (4%)
  blocking collectives  11.4 us (4%)
    ppermute x17, waiting for transfers between devices, swap(): return lax.ppermute(value, axis, [(i, i ^ offset) for i in range(count)])  107 us
    pallas_call x4, Pallas kernels, chunk_call(): pl.pallas_call(functools.partial(chunk_kernel, hi_count, zl_count), grid_...  58.3 us
    unnamed x68, local copies, waits for them, and re-layouts  21.1 us
    ppermute x17, starting transfers between devices, swap(): return lax.ppermute(value, axis, [(i, i ^ offset) for i in range(count)])  19.4 us
    all_to_all x4, starting transfers between devices, body(): own[stage] = lax.all_to_all(part, ('zl', 'narrow'), 0, 0, tiled=True)  18.2 us
    all_to_all x4, waiting for transfers between devices, body(): own[stage] = lax.all_to_all(part, ('zl', 'narrow'), 0, 0, tiled=True)  17.8 us
    pallas_call x1, Pallas kernels, pick_call(): pl.pallas_call(functools.partial(pick_kernel, len(blocks)), grid_spec=plt...  12.6 us
    convert_element_type x4, other arithmetic, sign_block(): return (2 * part - 1).astype(jnp.bfloat16)  11.9 us
  transfers between devices with their start and end apart: 23, of which 8 were waited for; matrix products, arithmetic and copies ran while one was open for 6% of the time, Pallas kernels for 19%

commit v1 on v0

--- a/solution.py
+++ b/solution.py
@@ -39,40 +39,42 @@
     return tile, [1, units - 2 - middle, middle, 1]
 
 
-def prep_kernel(real_blocks, zl_count, widths, in_ref, *out_refs):
+def prep_kernel(real_blocks, zl_count, spans, in_ref, *out_refs):
     block = pl.program_id(1) * zl_count + pl.program_id(0)
     keep = block < real_blocks
-    start = 0
-    for width, out_ref in zip(widths, out_refs):
-        value = in_ref[:, start : start + width]
+    for (start, stop), out_ref in zip(spans, out_refs):
+        value = in_ref[:, start:stop]
         out_ref[0] = jnp.where(keep, value, jnp.zeros_like(value))
-        start += width
-
-
-def prepare(cot, zl_count, narrow_count, widths):
+
+
+def prepare(cot, zl_count, narrow_count, col_dev, read, spans):
     tokens, hidden = cot.shape
-    col_dev = sum(widths)
     real_blocks = hidden // col_dev
+    stride = col_dev // read
     return pl.pallas_call(
-        functools.partial(prep_kernel, real_blocks, zl_count, widths),
+        functools.partial(prep_kernel, real_blocks, zl_count, spans),
         grid=(zl_count, narrow_count),
         in_specs=[
             pl.BlockSpec(
-                (tokens, col_dev),
-                lambda z, n: (0, jnp.minimum(n * zl_count + z, real_blocks - 1)),
+                (tokens, read),
+                lambda z, n: (0, jnp.minimum(n * zl_count + z, real_blocks - 1) * stride),
             )
         ],
         out_specs=[
-            pl.BlockSpec((1, tokens, width), lambda z, n: (z * narrow_count + n, 0, 0))
-            for width in widths
+            pl.BlockSpec(
+                (1, tokens, stop - start), lambda z, n: (z * narrow_count + n, 0, 0)
+            )
+            for start, stop in spans
         ],
         out_shape=[
-            jax.ShapeDtypeStruct((zl_count * narrow_count, tokens, width), cot.dtype)
-            for width in widths
+            jax.ShapeDtypeStruct(
+                (zl_count * narrow_count, tokens, stop - start), cot.dtype
+            )
+            for start, stop in spans
         ],
         compiler_params=pltpu.CompilerParams(vmem_limit_bytes=60 * MIB),
         cost_estimate=pl.CostEstimate(
-            flops=0, bytes_accessed=4 * cot.size, transcendentals=0
+            flops=0, bytes_accessed=4 * cot.size // stride, transcendentals=0
         ),
         name="cut_columns",
     )(cot)
@@ -251,8 +253,12 @@
     col_dev = col_shard // zl_count
     tile, chunks = plan_chunks(col_dev)
     tokens = token_shard * narrow_count // wide_count
-    cut = prepare(
-        out_cotangent[0, 0], zl_count, narrow_count, [tile * steps for steps in chunks]
+    edges = [tile * sum(chunks[:i]) for i in range(len(chunks) + 1)]
+    spans = list(zip(edges, edges[1:]))
+    cot = out_cotangent[0, 0]
+    cut = list(prepare(cot, zl_count, narrow_count, col_dev, edges[1], spans[:1]))
+    cut += prepare(
+        after(cot, cut[0]), zl_count, narrow_count, col_dev, col_dev, spans[1:]
     )
 
     own_xt = inputs[0].reshape(token_shard // tokens, tokens, rows).swapaxes(1, 2)
@@ -260,11 +266,9 @@
 
     row_mix = jnp.asarray(hadamard(rows), jnp.bfloat16)
     place = jnp.stack([hi, zl, core]).astype(jnp.int32)
-    edges = [tile * sum(chunks[:i]) for i in range(len(chunks) + 1)]
     count = len(chunks)
     own, far, signs, swapped = {}, {}, {}, {}
     blocks, xt = [], None
-    cut = list(cut)
     bits = sign_bits[0]
     samples = (row_pick[0], col_pick[0])
 
@@ -276,8 +280,7 @@
     for stage in range(count + 2):
         if stage < count:
             signs[stage] = [sign_block(d, stage) for d in range(zl_count)]
-            part = after(cut[stage], *signs[stage]) if stage > 1 else cut[stage]
-            own[stage] = lax.all_to_all(part, ("zl", "narrow"), 0, 0, tiled=True)
+            own[stage] = lax.all_to_all(cut[stage], ("zl", "narrow"), 0, 0, tiled=True)
         if 1 <= stage <= count:
             c = stage - 1
             far[c] = [swap(own[c], "hi", h) for h in range(1, hi_count)]
@@ -297,7 +300,7 @@
             )
             blocks.append(done.reshape(-1, zl_count * rows, LANES))
             place = after(place, done)
-        if stage == 2:
+        if stage == 3:
             row, col = samples
             block = (col // LANES) % (col_dev // LANES)
             row_in = (row // (2 * rows)) % zl_count * rows + row % rows

time: 309 us -> 305 us (0.987)
  Pallas kernels: 77.6 us -> 82.5 us
    pallas_call x1 -> x2, Pallas kernels: 6.75 us -> 11.4 us  [prepare(): pl.pallas_call(functools.partial(prep_kernel, real_blocks, zl_count, span...]
    all_to_all x4, waiting for transfers between devices: 17.8 us -> 13.1 us  [body(): own[stage] = lax.all_to_all(cut[stage], ('zl', 'narrow'), 0, 0, tiled=True)]
    unnamed x68 -> x58, local copies, waits for them, and re-layouts: 21.1 us -> 18.1 us
  transfers between devices with their start and end apart: 23 -> 23, of which waited for: 8 -> 8; matrix products, arithmetic and copies ran while one was open for 6% -> 6% of each run, Pallas kernels for 19% -> 21%
where the time goes in v1:
time: 305 us; the launch traced here: 304 us
  waiting for transfers between devices  122 us (40%)
  Pallas kernels  82.5 us (27%)
  starting transfers between devices  35.9 us (12%)
  local copies, waits for them, and re-layouts  22.7 us (7%)
  other arithmetic  16.5 us (5%)
  between operations  13.7 us (4%)
  blocking collectives  10.9 us (4%)
    ppermute x17, waiting for transfers between devices, swap(): return lax.ppermute(value, axis, [(i, i ^ offset) for i in range(count)])  109 us
    pallas_call x4, Pallas kernels, chunk_call(): pl.pallas_call(functools.partial(chunk_kernel, hi_count, zl_count), grid_...  58.6 us
    all_to_all x4, starting transfers between devices, body(): own[stage] = lax.all_to_all(cut[stage], ('zl', 'narrow'), 0, 0, tiled=True)  19.1 us
    unnamed x58, local copies, waits for them, and re-layouts  18.1 us
    ppermute x17, starting transfers between devices, swap(): return lax.ppermute(value, axis, [(i, i ^ offset) for i in range(count)])  16.7 us
    all_to_all x4, waiting for transfers between devices, body(): own[stage] = lax.all_to_all(cut[stage], ('zl', 'narrow'), 0, 0, tiled=True)  13.1 us
    pallas_call x1, Pallas kernels, pick_call(): pl.pallas_call(functools.partial(pick_kernel, len(blocks)), grid_spec=plt...  12.6 us
    pallas_call x2, Pallas kernels, prepare(): pl.pallas_call(functools.partial(prep_kernel, real_blocks, zl_count, span...  11.4 us
  transfers between devices with their start and end apart: 23, of which 8 were waited for; matrix products, arithmetic and copies ran while one was open for 6% of the time, Pallas kernels for 21%

profile of v1, /device:TPU:0, one launch (start us, length us, event | category | flops | bytes accessed | tf_op | source)
XLA Modules:
  0.0 303.9 jit_solution(5033164096285785442)
XLA Ops:
  8.9 3.1 %collective-permute-start = (bf16[2,512,512]{1,2,0:T(8,128)(2,1)}, bf16[2,512,512]{1,2,0:T(8,128)(2,1)S(1)}, u32[]{:S(2)}, u32[]{:S(2)}) collective-permute-start(bf16[2,512,512]{1,2,0:T(8,128)(2,1)} %bitcast.56), channel_id=1, source_target_pairs={{0,8},{8,0},{1,9},{9,1},{2,10},{10,2},{3,11},{11,3},{4,12},{12,4},... | collective-permute-start | bytes 3145736 | tf_op jit(solution)/shard_map/ppermute | solution.py:238
  12.0 4.7 %cut_columns.2 = bf16[8,128,256]{2,1,0:T(8,128)(2,1)} custom-call(bf16[128,14336]{1,0:T(8,128)(2,1)} %bitcast.50), custom_call_target="tpu_custom_call" | custom-call | bytes 917504 | tf_op jit(solution)/shard_map/cut_columns/pallas_call | solution.py:54
  16.7 3.7 %all-to-all-start = ((bf16[8,128,256]{2,1,0:T(8,128)(2,1)}), bf16[8,128,256]{2,1,0:T(8,128)(2,1)S(1)}, u32[]{:S(2)}, u32[]{:S(2)}) async-start(bf16[8,128,256]{2,1,0:T(8,128)(2,1)} %cut_columns.2), calls=%async_computation | async-start | bytes 1048576 | tf_op jit(solution)/shard_map/all_to_all | solution.py:283
  20.4 6.6 %cut_columns.3 = (bf16[8,128,768]{2,1,0:T(8,128)(2,1)}, bf16[8,128,768]{2,1,0:T(8,128)(2,1)}, bf16[8,128,256]{2,1,0:T(8,128)(2,1)}) custom-call(bf16[128,14336]{1,0:T(8,128)(2,1)} %bitcast.51), custom_call_target="tpu_custom_call" | custom-call | bytes 7340032 | tf_op jit(solution)/shard_map/cut_columns/pallas_call | solution.py:54
  29.1 13.1 %all-to-all-done = bf16[8,128,256]{2,1,0:T(8,128)(2,1)S(1)} async-done(((bf16[8,128,256]{2,1,0:T(8,128)(2,1)}), bf16[8,128,256]{2,1,0:T(8,128)(2,1)S(1)}, u32[]{:S(2)}, u32[]{:S(2)}) %all-to-all-start) | async-done | bytes 524320 | tf_op jit(solution)/shard_map/all_to_all | solution.py:283
  43.3 3.6 %all-to-all-start.1 = ((bf16[8,128,768]{2,1,0:T(8,128)(2,1)}), bf16[8,128,768]{2,1,0:T(8,128)(2,1)S(1)}, u32[]{:S(2)}, u32[]{:S(2)}) async-start(bf16[8,128,768]{2,1,0:T(8,128)(2,1)} %get-tuple-element.90), calls=%async_computation.1 | async-start | bytes 3145728 | tf_op jit(solution)/shard_map/all_to_all | solution.py:283
  49.3 2.7 collective-permute-start.1
  53.9 3.4 %add_convert_fusion.2 = (bf16[512,768]{1,0:T(8,128)(2,1)}, bf16[512,768]{1,0:T(8,128)(2,1)}) fusion(s32[512,4096]{1,0:T(8,128)} %bitcast.52, s32[]{:T(128)S(6)} %select_n.50, s32[]{:T(128)S(6)} %select_n.49), kind=kLoop, calls=%fused_computation.12 | loop fusion | flops 2359296 | bytes 4718600 | tf_op jit(solution)/shard_map/convert_element_type | solution.py:278
  57.3 24.8 %collective-permute-done.2.refs_7_ = bf16[512,256]{1,0:T(8,128)(2,1)} collective-permute-done((bf16[512,256]{1,0:T(8,128)(2,1)}, bf16[512,256]{1,0:T(8,128)(2,1)}, u32[]{:S(2)}, u32[]{:S(2)}) %collective-permute-start.2) | collective-permute-done | bytes 262176 | tf_op jit(solution)/shard_map/ppermute | solution.py:238
  82.2 4.3 %all-to-all-start.2 = ((bf16[8,128,768]{2,1,0:T(8,128)(2,1)}), bf16[8,128,768]{2,1,0:T(8,128)(2,1)}, u32[]{:S(2)}, u32[]{:S(2)}) async-start(bf16[8,128,768]{2,1,0:T(8,128)(2,1)} %get-tuple-element.101), calls=%async_computation.2 | async-start | bytes 3145728 | tf_op jit(solution)/shard_map/all_to_all | solution.py:283
  86.6 2.7 collective-permute-start.4
  91.1 3.5 %add_convert_fusion = (bf16[512,768]{1,0:T(8,128)(2,1)}, bf16[512,768]{1,0:T(8,128)(2,1)}) fusion(s32[512,4096]{1,0:T(8,128)} %bitcast.53, s32[]{:T(128)S(6)} %select_n.52, s32[]{:T(128)S(6)} %select_n.51), kind=kLoop, calls=%fused_computation.10 | loop fusion | flops 2359296 | bytes 4718600 | tf_op jit(solution)/shard_map/convert_element_type | solution.py:278
  94.6 57.9 %collective-permute-done.5.refs_7_ = bf16[512,768]{1,0:T(8,128)(2,1)} collective-permute-done((bf16[512,768]{1,0:T(8,128)(2,1)}, bf16[512,768]{1,0:T(8,128)(2,1)}, u32[]{:S(2)}, u32[]{:S(2)}) %collective-permute-start.5) | collective-permute-done | bytes 786464 | tf_op jit(solution)/shard_map/ppermute | solution.py:238
  152.6 5.6 %collective-permute-done.4 = bf16[8,128,768]{2,1,0:T(8,128)(2,1)} collective-permute-done((bf16[8,128,768]{2,1,0:T(8,128)(2,1)S(1)}, bf16[8,128,768]{2,1,0:T(8,128)(2,1)}, u32[]{:S(2)}, u32[]{:S(2)}) %collective-permute-start.4) | collective-permute-done | bytes 1572896 | tf_op jit(solution)/shard_map/ppermute | solution.py:238
  158.2 7.5 %all-to-all-start.3 = ((bf16[8,128,256]{2,1,0:T(8,128)(2,1)}), bf16[8,128,256]{2,1,0:T(8,128)(2,1)}, u32[]{:S(2)}, u32[]{:S(2)}) async-start(bf16[8,128,256]{2,1,0:T(8,128)(2,1)} %get-tuple-element.115), calls=%async_computation.3 | async-start | bytes 1048576 | tf_op jit(solution)/shard_map/all_to_all | solution.py:283
  167.8 4.7 %fusion.4.refs_4_ = bf16[8192,128]{1,0:T(8,128)(2,1)} fusion(s32[8192]{0:T(1024)S(1)} %bitcast.58, s32[128]{0:T(128)S(1)} %iota_add_fusion, s32[8192]{0:T(1024)S(1)} %get-tuple-element.175), kind=kLoop, calls=%fused_computation.9 | loop fusion | flops 16777216 | bytes 2163200 | tf_op jit(solution)/shard_map/convert_element_type | solution.py:312
  181.1 7.6 %gradient_rows.4 = f32[2,2,512,128]{3,2,1,0:T(8,128)S(1)} custom-call(s32[3]{0:T(128)S(1)} %pad_add_fusion.place_ref, bf16[8,512,512]{2,1,0:T(8,128)(2,1)S(1)} %copy-done, bf16[8,512,512]{2,1,0:T(8,128)(2,1)S(1)} %copy-done.2, bf16[2,512,256]{2,1,0:T(8,128)(2,1)S(1)} %bitcast.41, bf16[2,512,256]{2,1,0:T(8,128)(2,1)S(1)} %bitcast.44, ...), custom_call_target="tpu_custom_call" | custom-call | flops 134217728 | bytes 1048576 | tf_op jit(solution)/shard_map/gradient_rows/pallas_call | solution.py:121
  191.3 21.6 %gradient_rows.5 = f32[6,2,512,128]{3,2,1,0:T(8,128)S(1)} custom-call(s32[3]{0:T(128)S(1)} %pad_add_fusion.place_ref, bf16[8,512,512]{2,1,0:T(8,128)(2,1)} %all-gather.3.cloned.1.call-done.refs_0_, bf16[8,512,512]{2,1,0:T(8,128)(2,1)} %all-gather.5.cloned.1.call-done.refs_1_, bf16[2,512,768]{2,1,0:T(8,128)(2,1)S(1)} %bitcast.38, ...), custom_call_target="tpu_custom_call" | custom-call | flops 402653184 | bytes 3145728 | tf_op jit(solution)/shard_map/gradient_rows/pallas_call | solution.py:121
  212.9 2.7 collective-permute-done.9.refs_7_
  215.6 14.3 %collective-permute-done.8 = bf16[8,128,768]{2,1,0:T(8,128)(2,1)} collective-permute-done((bf16[8,128,768]{2,1,0:T(8,128)(2,1)}, bf16[8,128,768]{2,1,0:T(8,128)(2,1)}, u32[]{:S(2)}, u32[]{:S(2)}) %collective-permute-start.8) | collective-permute-done | bytes 1572896 | tf_op jit(solution)/shard_map/ppermute | solution.py:238
  238.3 21.9 %gradient_rows.6 = f32[6,2,512,128]{3,2,1,0:T(8,128)S(1)} custom-call(s32[3]{0:T(128)S(1)} %pad_add_fusion.place_ref, bf16[8,512,512]{2,1,0:T(8,128)(2,1)} %all-gather.3.cloned.1.call-done.refs_0_, bf16[8,512,512]{2,1,0:T(8,128)(2,1)} %all-gather.5.cloned.1.call-done.refs_1_, bf16[2,512,768]{2,1,0:T(8,128)(2,1)} %bitcast.22.refs_2_, ...), custom_call_target="tpu_custom_call" | custom-call | flops 402653184 | bytes 3145728 | tf_op jit(solution)/shard_map/gradient_rows/pallas_call | solution.py:121
  265.4 7.5 %gradient_rows.7 = f32[2,2,512,128]{3,2,1,0:T(8,128)S(1)} custom-call(s32[3]{0:T(128)S(1)} %pad_add_fusion.place_ref, bf16[8,512,512]{2,1,0:T(8,128)(2,1)S(1)} %copy-done.1, bf16[8,512,512]{2,1,0:T(8,128)(2,1)S(1)} %copy-done.3, bf16[2,512,256]{2,1,0:T(8,128)(2,1)} %bitcast.27.refs_2_, bf16[2,512,256]{2,1,0:T(8,128)(2,1)S(1)} %bitcast.46, ...), custom_call_target="tpu_custom_call" | custom-call | flops 134217728 | bytes 1048576 | tf_op jit(solution)/shard_map/gradient_rows/pallas_call | solution.py:121
  273.0 12.6 %pick_samples.1 = f32[64,128]{1,0:T(8,128)S(1)} custom-call(s32[8192]{0:T(1024)S(1)} %get-tuple-element.161.index_ref, f32[2,1024,128]{2,1,0:T(8,128)S(1)} %bitcast.39, f32[6,1024,128]{2,1,0:T(8,128)S(1)} %bitcast.36, f32[6,1024,128]{2,1,0:T(8,128)S(1)} %bitcast.37, f32[2,1024,128]{2,1,0:T(8,128)S(1)} %bitcast.40, bf16[8192,128]{1,0:T(8,128)(2,1)S(1)} %copy-done.9), custom_call_target="tpu_custom_call" | custom-call | flops 16777216 | bytes 8388608 | tf_op jit(solution)/shard_map/pick_samples/pallas_call | solution.py:199
  285.6 10.9 %all_to_all.29 = f32[32,1,256]{2,1,0:T(1,128)S(1)} all-to-all(f32[32,1,256]{2,1,0:T(1,128)S(1)} %bitcast.49), channel_id=1, replica_groups=mesh['hi'=2,'zl'=2,'core'=2,'narrow'=4] {'hi','zl','core','narrow'}, dimensions={0} | all-to-all | bytes 65536 | tf_op jit(solution)/shard_map/all_to_all | solution.py:322
  (102 shorter events, 39.2 us)
Async XLA Ops:
  6.5 168.0 %all-gather.3.cloned.1.call-start = ((), (), s32[]{:S(2)}) async-start(), calls=%async_computation.5 | async-start | bytes 5242880 | tf_op jit(solution)/shard_map/all_gather | solution.py:317
  8.9 33.4 %collective-permute-start = (bf16[2,512,512]{1,2,0:T(8,128)(2,1)}, bf16[2,512,512]{1,2,0:T(8,128)(2,1)S(1)}, u32[]{:S(2)}, u32[]{:S(2)}) collective-permute-start(bf16[2,512,512]{1,2,0:T(8,128)(2,1)} %bitcast.56), channel_id=1, source_target_pairs={{0,8},{8,0},{1,9},{9,1},{2,10},{10,2},{3,11},{11,3},{4,12},{12,4},... | collective-permute-start | bytes 3145736 | tf_op jit(solution)/shard_map/ppermute | solution.py:238
  16.7 25.6 %all-to-all-start = ((bf16[8,128,256]{2,1,0:T(8,128)(2,1)}), bf16[8,128,256]{2,1,0:T(8,128)(2,1)S(1)}, u32[]{:S(2)}, u32[]{:S(2)}) async-start(bf16[8,128,256]{2,1,0:T(8,128)(2,1)} %cut_columns.2), calls=%async_computation | async-start | bytes 1048576 | tf_op jit(solution)/shard_map/all_to_all | solution.py:283
  43.3 38.9 %all-to-all-start.1 = ((bf16[8,128,768]{2,1,0:T(8,128)(2,1)}), bf16[8,128,768]{2,1,0:T(8,128)(2,1)S(1)}, u32[]{:S(2)}, u32[]{:S(2)}) async-start(bf16[8,128,768]{2,1,0:T(8,128)(2,1)} %get-tuple-element.90), calls=%async_computation.1 | async-start | bytes 3145728 | tf_op jit(solution)/shard_map/all_to_all | solution.py:283
  46.9 127.7 %all-gather.5.cloned.1.call-start = ((), (), s32[]{:S(2)}) async-start(), calls=%async_computation.6 | async-start | bytes 5242880 | tf_op jit(solution)/shard_map/all_gather | solution.py:317
  49.2 32.9 %collective-permute-start.3 = (bf16[8,128,256]{2,1,0:T(8,128)(2,1)S(1)}, bf16[8,128,256]{2,1,0:T(8,128)(2,1)S(1)}, u32[]{:S(2)}, u32[]{:S(2)}) collective-permute-start(bf16[8,128,256]{2,1,0:T(8,128)(2,1)S(1)} %all-to-all-done), channel_id=1, source_target_pairs={{0,4},{4,0},{1,5},{5,1},{2,6},{6,2},{3,7},{7,3},{8,12},{12,8},{9,1... | collective-permute-start | bytes 1572872 | tf_op jit(solution)/shard_map/ppermute | solution.py:238
  49.3 32.9 %collective-permute-start.1 = (bf16[8,128,256]{2,1,0:T(8,128)(2,1)S(1)}, bf16[8,128,256]{2,1,0:T(8,128)(2,1)S(1)}, u32[]{:S(2)}, u32[]{:S(2)}) collective-permute-start(bf16[8,128,256]{2,1,0:T(8,128)(2,1)S(1)} %all-to-all-done), channel_id=1, source_target_pairs={{0,16},{16,0},{1,17},{17,1},{2,18},{18,2},{3,19},{19,3},{4,20},{20... | collective-permute-start | bytes 1572872 | tf_op jit(solution)/shard_map/ppermute | solution.py:238
  52.0 30.2 %collective-permute-start.2 = (bf16[512,256]{1,0:T(8,128)(2,1)}, bf16[512,256]{1,0:T(8,128)(2,1)}, u32[]{:S(2)}, u32[]{:S(2)}) collective-permute-start(bf16[512,256]{1,0:T(8,128)(2,1)} %get-tuple-element.95), channel_id=1, source_target_pairs={{0,8},{8,0},{1,9},{9,1},{2,10},{10,2},{3,11},{11,3},{4,12},{12,4},... | collective-permute-start | bytes 786440 | tf_op jit(solution)/shard_map/ppermute | solution.py:238
  82.2 76.0 %all-to-all-start.2 = ((bf16[8,128,768]{2,1,0:T(8,128)(2,1)}), bf16[8,128,768]{2,1,0:T(8,128)(2,1)}, u32[]{:S(2)}, u32[]{:S(2)}) async-start(bf16[8,128,768]{2,1,0:T(8,128)(2,1)} %get-tuple-element.101), calls=%async_computation.2 | async-start | bytes 3145728 | tf_op jit(solution)/shard_map/all_to_all | solution.py:283
  86.5 66.0 %collective-permute-start.7 = (bf16[8,128,768]{2,1,0:T(8,128)(2,1)S(1)}, bf16[8,128,768]{2,1,0:T(8,128)(2,1)}, u32[]{:S(2)}, u32[]{:S(2)}) collective-permute-start(bf16[8,128,768]{2,1,0:T(8,128)(2,1)S(1)} %all-to-all-done.1), channel_id=1, source_target_pairs={{0,4},{4,0},{1,5},{5,1},{2,6},{6,2},{3,7},{7,3},{8,12},{12,8},{9,1... | collective-permute-start | bytes 4718600 | tf_op jit(solution)/shard_map/ppermute | solution.py:238
  86.6 71.6 %collective-permute-start.4 = (bf16[8,128,768]{2,1,0:T(8,128)(2,1)S(1)}, bf16[8,128,768]{2,1,0:T(8,128)(2,1)}, u32[]{:S(2)}, u32[]{:S(2)}) collective-permute-start(bf16[8,128,768]{2,1,0:T(8,128)(2,1)S(1)} %all-to-all-done.1), channel_id=1, source_target_pairs={{0,16},{16,0},{1,17},{17,1},{2,18},{18,2},{3,19},{19,3},{4,20},{20... | collective-permute-start | bytes 4718600 | tf_op jit(solution)/shard_map/ppermute | solution.py:238
  89.3 63.3 %collective-permute-start.5 = (bf16[512,768]{1,0:T(8,128)(2,1)}, bf16[512,768]{1,0:T(8,128)(2,1)}, u32[]{:S(2)}, u32[]{:S(2)}) collective-permute-start(bf16[512,768]{1,0:T(8,128)(2,1)} %get-tuple-element.109), channel_id=1, source_target_pairs={{0,8},{8,0},{1,9},{9,1},{2,10},{10,2},{3,11},{11,3},{4,12},{12,4},... | collective-permute-start | bytes 2359304 | tf_op jit(solution)/shard_map/ppermute | solution.py:238
  91.1 3.5 %collective-permute-start.6 = (bf16[8,128,256]{2,1,0:T(8,128)(2,1)S(1)}, bf16[8,128,256]{2,1,0:T(8,128)(2,1)}, u32[]{:S(2)}, u32[]{:S(2)}) collective-permute-start(bf16[8,128,256]{2,1,0:T(8,128)(2,1)S(1)} %collective-permute-done.1), channel_id=1, source_target_pairs={{0,4},{4,0},{1,5},{5,1},{2,6},{6,2},{3,7},{7,3},{8,12},{12,8},{9,1... | collective-permute-start | bytes 1572872 | tf_op jit(solution)/shard_map/ppermute | solution.py:238
  91.1 83.5 %copy-start.6 = (bf16[512,512]{1,0:T(8,128)(2,1)S(1)}, bf16[512,512]{1,0:T(8,128)(2,1)}, u32[]{:S(2)}) copy-start(bf16[512,512]{1,0:T(8,128)(2,1)} %constant.133.clone.refs_8_) | copy-start | bytes 1572868
  158.2 57.4 %collective-permute-start.11 = (bf16[8,128,768]{2,1,0:T(8,128)(2,1)}, bf16[8,128,768]{2,1,0:T(8,128)(2,1)}, u32[]{:S(2)}, u32[]{:S(2)}) collective-permute-start(bf16[8,128,768]{2,1,0:T(8,128)(2,1)} %all-to-all-done.2), channel_id=1, source_target_pairs={{0,4},{4,0},{1,5},{5,1},{2,6},{6,2},{3,7},{7,3},{8,12},{12,8},{9,1... | collective-permute-start | bytes 4718600 | tf_op jit(solution)/shard_map/ppermute | solution.py:238
  158.2 71.7 %collective-permute-start.8 = (bf16[8,128,768]{2,1,0:T(8,128)(2,1)}, bf16[8,128,768]{2,1,0:T(8,128)(2,1)}, u32[]{:S(2)}, u32[]{:S(2)}) collective-permute-start(bf16[8,128,768]{2,1,0:T(8,128)(2,1)} %all-to-all-done.2), channel_id=1, source_target_pairs={{0,16},{16,0},{1,17},{17,1},{2,18},{18,2},{3,19},{19,3},{4,20},{20... | collective-permute-start | bytes 4718600 | tf_op jit(solution)/shard_map/ppermute | solution.py:238
  158.2 57.4 %all-to-all-start.3 = ((bf16[8,128,256]{2,1,0:T(8,128)(2,1)}), bf16[8,128,256]{2,1,0:T(8,128)(2,1)}, u32[]{:S(2)}, u32[]{:S(2)}) async-start(bf16[8,128,256]{2,1,0:T(8,128)(2,1)} %get-tuple-element.115), calls=%async_computation.3 | async-start | bytes 1048576 | tf_op jit(solution)/shard_map/all_to_all | solution.py:283
  165.7 49.9 %collective-permute-start.9 = (bf16[512,768]{1,0:T(8,128)(2,1)}, bf16[512,768]{1,0:T(8,128)(2,1)}, u32[]{:S(2)}, u32[]{:S(2)}) collective-permute-start(bf16[512,768]{1,0:T(8,128)(2,1)} %get-tuple-element.126), channel_id=1, source_target_pairs={{0,8},{8,0},{1,9},{9,1},{2,10},{10,2},{3,11},{11,3},{4,12},{12,4},... | collective-permute-start | bytes 2359304 | tf_op jit(solution)/shard_map/ppermute | solution.py:238
  167.7 20.9 %collective-permute-start.10 = (bf16[8,128,768]{2,1,0:T(8,128)(2,1)}, bf16[8,128,768]{2,1,0:T(8,128)(2,1)S(1)}, u32[]{:S(2)}, u32[]{:S(2)}) collective-permute-start(bf16[8,128,768]{2,1,0:T(8,128)(2,1)} %collective-permute-done.4), channel_id=1, source_target_pairs={{0,4},{4,0},{1,5},{5,1},{2,6},{6,2},{3,7},{7,3},{8,12},{12,8},{9,1... | collective-permute-start | bytes 4718600 | tf_op jit(solution)/shard_map/ppermute | solution.py:238
  229.9 3.6 %collective-permute-start.14 = (bf16[8,128,768]{2,1,0:T(8,128)(2,1)}, bf16[8,128,768]{2,1,0:T(8,128)(2,1)S(1)}, u32[]{:S(2)}, u32[]{:S(2)}) collective-permute-start(bf16[8,128,768]{2,1,0:T(8,128)(2,1)} %collective-permute-done.8), channel_id=1, source_target_pairs={{0,4},{4,0},{1,5},{5,1},{2,6},{6,2},{3,7},{7,3},{8,12},{12,8},{9,1... | collective-permute-start | bytes 4718600 | tf_op jit(solution)/shard_map/ppermute | solution.py:238
  229.9 32.6 %collective-permute-start.15 = (bf16[8,128,256]{2,1,0:T(8,128)(2,1)}, bf16[8,128,256]{2,1,0:T(8,128)(2,1)S(1)}, u32[]{:S(2)}, u32[]{:S(2)}) collective-permute-start(bf16[8,128,256]{2,1,0:T(8,128)(2,1)} %all-to-all-done.3), channel_id=1, source_target_pairs={{0,4},{4,0},{1,5},{5,1},{2,6},{6,2},{3,7},{7,3},{8,12},{12,8},{9,1... | collective-permute-start | bytes 1572872 | tf_op jit(solution)/shard_map/ppermute | solution.py:238
  230.4 32.1 %collective-permute-start.12 = (bf16[8,128,256]{2,1,0:T(8,128)(2,1)}, bf16[8,128,256]{2,1,0:T(8,128)(2,1)S(1)}, u32[]{:S(2)}, u32[]{:S(2)}) collective-permute-start(bf16[8,128,256]{2,1,0:T(8,128)(2,1)} %all-to-all-done.3), channel_id=1, source_target_pairs={{0,16},{16,0},{1,17},{17,1},{2,18},{18,2},{3,19},{19,3},{4,20},{20... | collective-permute-start | bytes 1572872 | tf_op jit(solution)/shard_map/ppermute | solution.py:238
  230.4 31.4 %collective-permute-start.13 = (bf16[512,256]{1,0:T(8,128)(2,1)}, bf16[512,256]{1,0:T(8,128)(2,1)S(1)}, u32[]{:S(2)}, u32[]{:S(2)}) collective-permute-start(bf16[512,256]{1,0:T(8,128)(2,1)} %get-tuple-element.142), channel_id=1, source_target_pairs={{0,8},{8,0},{1,9},{9,1},{2,10},{10,2},{3,11},{11,3},{4,12},{12,4},... | collective-permute-start | bytes 786440 | tf_op jit(solution)/shard_map/ppermute | solution.py:238
  262.6 1.9 collective-permute-start.16
  (28 other events, 340.0 us)
Sparse Core Ops, SparseCore 0:
  9.2 76.4 all-gather.2
  87.6 60.0 all-gather.4
